TPU v7x, 512 devices: a whole 4x4x16 slice. The times are simulated.
512 devices in a mesh: slab: 512 (over y, z, x, core).
Axes of the slice: x: 4, y: 4, z: 16, core: 2. Of those that a mesh axis runs over, the one named last changes fastest.
Arguments:
- start_vectors: float32 [32, 1024, 4096], P(None, 'slab'), may hold values from -120 to 120, as said below
- materials: int32 [1024, 4096], P('slab'), may hold values from 0 to 7
- conduct_table: float32 [8], replicated, may hold values from 0.1 to 10
- aggregate_ids: int32 [8192], P('slab'), may hold values from 0 to 4095, never falling along the last dimension, each value on 1 to 16 neighbouring positions
Outputs:
- prolongator: float32 [32, 1024, 4096], P(None, 'slab')
- coarse_factors: float32 [8192, 32, 32], P('slab')
Inputs may be any that keep to these rules, and one draw needn't show every extreme that they name: `start_vectors`: built from normal or uniform values; rows differ in scale. `aggregate_ids`: aggregate numbers never fall along the blocks; each aggregate is 1 to 16 consecutive blocks, and one is exactly 16.
All inputs are finite; a program needn't handle non-finite values.
Results may differ from a plain program's by a relative error of at most 0.0003.
Values sent between devices are 32-bit elements; how exact they have to be, the bound alone decides.
A program may use at most 64 MiB of HBM per device.

v0:
```python
import jax
import jax.numpy as jnp
from jax import lax
from jax.sharding import PartitionSpec as P

BLKR = 512
NX = 256
SWEEPS = 4


relax_weight = 2.0 / 3.0
epsilon = 1e-06


def with_halo(cells, sides, width):
    for axis, dim in sides:
        count = lax.axis_size(axis)
        ends = count - 1
        head = lax.slice_in_dim(cells, 0, width, axis=dim)
        tail = lax.slice_in_dim(cells, cells.shape[dim] - width, cells.shape[dim], axis=dim)
        cells = jnp.concatenate(
            [
                lax.ppermute(tail, axis, [(i, (i + 1) % count) for i in range(ends)]),
                cells,
                lax.ppermute(head, axis, [((i + 1) % count, i) for i in range(ends)]),
            ],
            axis=dim,
        )
    return cells


def shifted(values, offset, x_mask):
    padding = jnp.zeros(values.shape[:-1] + (abs(offset),), values.dtype)
    if offset > 0:
        moved_vals = jnp.concatenate([values[..., offset:], padding], axis=-1)
    else:
        moved_vals = jnp.concatenate([padding, values[..., :offset]], axis=-1)
    return moved_vals * x_mask


def plane_masks(plane_len):
    xpos = jnp.arange(plane_len) % NX
    west = (xpos > 0).astype(jnp.float32)
    east = (xpos < NX - 1).astype(jnp.float32)
    return (west, east, jnp.ones((plane_len,), jnp.float32))


def face_coef(cond, other):
    return jnp.where(other > 0.0, 2.0 * cond * other / (cond + other), cond)


def coefficients(cond_ext):
    west, east, unity = plane_masks(cond_ext.shape[-1])
    inner = cond_ext[1:-1]
    coef_down = face_coef(inner, cond_ext[:-2])
    coef_up = face_coef(inner, cond_ext[2:])
    coef_west = face_coef(inner, shifted(inner, -1, west))
    coef_east = face_coef(inner, shifted(inner, 1, east))
    coef_south = face_coef(inner, shifted(inner, -NX, unity))
    coef_north = face_coef(inner, shifted(inner, NX, unity))
    diag_sum = coef_down + coef_up + coef_west + coef_east + coef_south + coef_north
    exists = inner > 0.0
    diag_safe = jnp.where(exists, diag_sum, 1.0)
    return (coef_down, coef_up, coef_west, coef_east, coef_south, coef_north, diag_safe, exists)


def jacobi_step(extended, coefs):
    west, east, unity = plane_masks(extended.shape[-1])
    inner = extended[:, 1:-1]
    neigh = coefs[0] * extended[:, :-2] + coefs[1] * extended[:, 2:]
    neigh = neigh + coefs[2] * shifted(inner, -1, west) + coefs[3] * shifted(inner, 1, east)
    neigh = neigh + coefs[4] * shifted(inner, -NX, unity) + coefs[5] * shifted(inner, NX, unity)
    return inner - relax_weight * (coefs[6] * inner - neigh) / coefs[6]


def test_rims(vectors, width):
    return with_halo(vectors, (("slab", 1),), width)


def root_means(vectors, cell_count):
    local_sq = jnp.sum(vectors * vectors, axis=(1, 2))
    total_sq = lax.psum(local_sq, "slab")
    return jnp.sqrt(total_sq / cell_count + epsilon)


def to_blocks(vectors, block_count):
    return jnp.transpose(vectors.reshape(vectors.shape[0], block_count, -1), (1, 0, 2))


def factor(blocks, agg_ids, nearby_ids):
    block_count, width = (blocks.shape[0], blocks.shape[1])
    grams = jnp.einsum("bkr,blr->bkl", blocks, blocks, precision=lax.Precision.HIGHEST) / BLKR
    flat = grams.reshape(block_count, width * width)
    same_agg = (agg_ids[:, None] == agg_ids[None, :]).astype(jnp.float32)
    local_sums = jnp.dot(
        same_agg, flat, precision=lax.Precision.HIGHEST, preferred_element_type=jnp.float32
    )
    edge_sums = jnp.stack([local_sums[0], local_sums[-1]])
    edge_rims = with_halo(edge_sums, (("slab", 0),), 1)
    left_match = (agg_ids == nearby_ids[0]).astype(jnp.float32)[:, None]
    right_match = (agg_ids == nearby_ids[-1]).astype(jnp.float32)[:, None]
    gram_sum = local_sums + left_match * edge_rims[0] + right_match * edge_rims[3]
    return jnp.linalg.cholesky(gram_sum.reshape(block_count, width, width))


def local(start_vectors, materials, conduct_table, aggregate_ids):
    depth_width = 1
    material_range = jnp.arange(conduct_table.shape[0])[:, None, None]
    conduct = jnp.sum(
        jnp.where(materials[None] == material_range, conduct_table[:, None, None], 0.0), axis=0
    )
    nearby_ids = with_halo(aggregate_ids, (("slab", 0),), 1)
    cond_ext = with_halo(conduct, (("slab", 0),), depth_width)
    coefs = coefficients(cond_ext)
    vectors = start_vectors
    for sweep in range(SWEEPS):
        vectors = jacobi_step(test_rims(vectors, 1), coefs)
    cell_count = lax.axis_size("slab") * vectors.shape[1] * vectors.shape[2]
    block_count = aggregate_ids.shape[0]
    root_mean = root_means(vectors, cell_count)
    blocks = to_blocks(vectors / root_mean[:, None, None], block_count)
    lower_fac = factor(blocks, aggregate_ids, nearby_ids)
    solved = lax.linalg.triangular_solve(lower_fac, blocks, left_side=True, lower=True)
    coarse = jnp.transpose(lower_fac, (0, 2, 1))
    prolongator = jnp.transpose(solved, (1, 0, 2)).reshape(vectors.shape)
    return (prolongator, coarse)


def solution(mesh):
    return jax.shard_map(
        local,
        mesh=mesh,
        in_specs=(P(None, "slab", None), P("slab", None), P(), P("slab")),
        out_specs=(P(None, "slab", None), P("slab", None, None)),
        check_vma=False,
    )
```

profile of v0, /device:TPU:8, one launch (start us, length us, event | category | flops | bytes accessed | tf_op | source)
XLA Modules:
  0.0 304.7 jit_solution(6113176650762822115)
XLA Ops:
  0.6 0.9 select_reduce_fusion.1
  1.6 1.9 collective-permute-start
  3.5 12.9 %collective-permute-start.1 = (f32[1,4096]{1,0:T(1,128)S(1)}, f32[1,4096]{1,0:T(1,128)S(1)}, u32[]{:S(2)}, u32[]{:S(2)}) collective-permute-start(f32[1,4096]{1,0:T(1,128)S(1)} %get-tuple-element.51), channel_id=1, source_target_pairs={{1,0},{2,1},{3,2},{4,3},{5,4},{6,5},{7,6},{8,7},{9,8},{10,9},{11,1... | collective-permute-start | bytes 49160 | tf_op jit(solution)/shard_map/ppermute | solution.py:25
  16.5 1.8 copy.56
  18.4 1.9 collective-permute-start.2
  20.3 7.9 %collective-permute-start.3 = (f32[32,1,4096]{2,0,1:T(8,128)S(1)}, f32[32,1,4096]{2,0,1:T(8,128)S(1)}, u32[]{:S(2)}, u32[]{:S(2)}) collective-permute-start(f32[32,1,4096]{2,0,1:T(8,128)S(1)} %get-tuple-element.42), channel_id=1, source_target_pairs={{1,0},{2,1},{3,2},{4,3},{5,4},{6,5},{7,6},{8,7},{9,8},{10,9},{11,1... | collective-permute-start | bytes 1572872 | tf_op jit(solution)/shard_map/ppermute | solution.py:25
  28.2 0.6 fusion.77
  28.8 1.9 collective-permute-start.10
  30.8 0.3 fusion.70
  31.2 0.1 fusion.71
  31.4 7.9 %collective-permute-start.12 = (s32[1]{0:T(128)}, s32[1]{0:T(128)}, u32[]{:S(2)}, u32[]{:S(2)}) collective-permute-start(s32[1]{0:T(128)} %get-tuple-element.58), channel_id=1, source_target_pairs={{1,0},{2,1},{3,2},{4,3},{5,4},{6,5},{7,6},{8,7},{9,8},{10,9},{11,1... | collective-permute-start | bytes 20 | tf_op jit(solution)/shard_map/ppermute | solution.py:25
  39.3 0.3 compare_select_fusion.6
  39.5 0.8 fusion.42
  40.3 0.3 fusion.67
  40.8 1.9 collective-permute-start.4
  42.7 7.9 %collective-permute-start.5 = (f32[32,1,4096]{2,0,1:T(8,128)S(1)}, f32[32,1,4096]{2,0,1:T(8,128)S(1)}, u32[]{:S(2)}, u32[]{:S(2)}) collective-permute-start(f32[32,1,4096]{2,0,1:T(8,128)S(1)} %get-tuple-element.36), channel_id=1, source_target_pairs={{1,0},{2,1},{3,2},{4,3},{5,4},{6,5},{7,6},{8,7},{9,8},{10,9},{11,1... | collective-permute-start | bytes 1572872 | tf_op jit(solution)/shard_map/ppermute | solution.py:25
  50.7 4.8 %collective-permute-done.4 = f32[32,1,4096]{2,0,1:T(8,128)S(1)} collective-permute-done((f32[32,1,4096]{2,0,1:T(8,128)S(1)}, f32[32,1,4096]{2,0,1:T(8,128)S(1)}, u32[]{:S(2)}, u32[]{:S(2)}) %collective-permute-start.4) | collective-permute-done | bytes 524320 | tf_op jit(solution)/shard_map/ppermute | solution.py:23
  55.5 1.8 collective-permute-done.5
  57.2 0.8 fusion.31
  58.0 0.4 fusion.64
  58.4 1.9 collective-permute-start.6
  60.4 8.0 %collective-permute-start.7 = (f32[32,1,4096]{2,0,1:T(8,128)S(1)}, f32[32,1,4096]{2,0,1:T(8,128)S(1)}, u32[]{:S(2)}, u32[]{:S(2)}) collective-permute-start(f32[32,1,4096]{2,0,1:T(8,128)S(1)} %get-tuple-element.30), channel_id=1, source_target_pairs={{1,0},{2,1},{3,2},{4,3},{5,4},{6,5},{7,6},{8,7},{9,8},{10,9},{11,1... | collective-permute-start | bytes 1572872 | tf_op jit(solution)/shard_map/ppermute | solution.py:25
  68.5 4.8 %collective-permute-done.6 = f32[32,1,4096]{2,0,1:T(8,128)S(1)} collective-permute-done((f32[32,1,4096]{2,0,1:T(8,128)S(1)}, f32[32,1,4096]{2,0,1:T(8,128)S(1)}, u32[]{:S(2)}, u32[]{:S(2)}) %collective-permute-start.6) | collective-permute-done | bytes 524320 | tf_op jit(solution)/shard_map/ppermute | solution.py:23
  73.3 1.8 collective-permute-done.7
  75.1 0.8 fusion.20
  75.9 0.3 fusion.62
  76.3 1.9 collective-permute-start.8
  78.2 8.0 %collective-permute-start.9 = (f32[32,1,4096]{2,0,1:T(8,128)S(1)}, f32[32,1,4096]{2,0,1:T(8,128)S(1)}, u32[]{:S(2)}, u32[]{:S(2)}) collective-permute-start(f32[32,1,4096]{2,0,1:T(8,128)S(1)} %get-tuple-element.20), channel_id=1, source_target_pairs={{1,0},{2,1},{3,2},{4,3},{5,4},{6,5},{7,6},{8,7},{9,8},{10,9},{11,1... | collective-permute-start | bytes 1572872 | tf_op jit(solution)/shard_map/ppermute | solution.py:25
  86.4 4.8 %collective-permute-done.8 = f32[32,1,4096]{2,0,1:T(8,128)S(1)} collective-permute-done((f32[32,1,4096]{2,0,1:T(8,128)S(1)}, f32[32,1,4096]{2,0,1:T(8,128)S(1)}, u32[]{:S(2)}, u32[]{:S(2)}) %collective-permute-start.8) | collective-permute-done | bytes 524320 | tf_op jit(solution)/shard_map/ppermute | solution.py:23
  91.2 1.8 collective-permute-done.9
  92.9 1.0 multiply_reduce_fusion
  93.9 103.4 %psum.7 = f32[32]{0:T(128)S(1)} all-reduce(f32[32]{0:T(128)S(1)} %get-tuple-element.12), channel_id=1, replica_groups=mesh['slab'=512] {'slab'}, use_global_device_ids=true, to_apply=%region_2.3 | all-reduce | flops 32 | bytes 256 | tf_op jit(solution)/shard_map/psum | solution.py:82
  197.3 0.2 broadcast_divide_fusion
  197.5 0.8 copy.57
  198.3 0.9 reshape.70
  199.2 2.1 convolution_multiply_fusion
  201.3 0.1 reshape.71
  201.4 0.2 fusion.56
  201.7 1.9 collective-permute-start.11
  203.6 7.9 %collective-permute-start.13 = (f32[1,1024]{1,0:T(1,128)S(1)}, f32[1,1024]{1,0:T(1,128)S(1)}, u32[]{:S(2)}, u32[]{:S(2)}) collective-permute-start(f32[1,1024]{1,0:T(1,128)S(1)} %get-tuple-element.46), channel_id=1, source_target_pairs={{1,0},{2,1},{3,2},{4,3},{5,4},{6,5},{7,6},{8,7},{9,8},{10,9},{11,1... | collective-permute-start | bytes 12296 | tf_op jit(solution)/shard_map/ppermute | solution.py:25
  211.5 1.3 compare_convert_fusion.1
  213.0 0.1 copy.60
  213.2 46.9 %custom-call.7 = f32[16,32,32]{2,1,0:T(8,128)S(1)} custom-call(f32[16,32,32]{2,1,0:T(8,128)S(1)} %fusion.47), custom_call_target="Cholesky" | custom-call | tf_op jit(solution)/shard_map/jit(cholesky)/cholesky | solution.py:103
  260.3 39.4 %custom-call.8 = f32[16,1,32,32]{2,3,1,0:T(8,128)S(1)} custom-call(f32[16,1,32,32]{3,2,1,0:T(8,128)S(1)} %get-tuple-element.44), custom_call_target="InvertDiagBlocksLowerTriangular" | custom-call | tf_op jit(solution)/shard_map/triangular_solve | solution.py:123
  299.7 1.6 convolution_bitcast_fusion
  301.4 0.6 copy.63
  302.0 1.9 reshape.73
  303.8 0.8 copy.64
  (31 shorter events, 1.4 us)
Async XLA Ops:
  1.6 29.8 %collective-permute-start = (f32[1,4096]{1,0:T(1,128)S(1)}, f32[1,4096]{1,0:T(1,128)S(1)}, u32[]{:S(2)}, u32[]{:S(2)}) collective-permute-start(f32[1,4096]{1,0:T(1,128)S(1)} %get-tuple-element.52), channel_id=1, source_target_pairs={{0,1},{1,2},{2,3},{3,4},{4,5},{5,6},{6,7},{7,8},{8,9},{9,10},{10,1... | collective-permute-start | bytes 49160 | tf_op jit(solution)/shard_map/ppermute | solution.py:23
  3.5 35.7 %collective-permute-start.1 = (f32[1,4096]{1,0:T(1,128)S(1)}, f32[1,4096]{1,0:T(1,128)S(1)}, u32[]{:S(2)}, u32[]{:S(2)}) collective-permute-start(f32[1,4096]{1,0:T(1,128)S(1)} %get-tuple-element.51), channel_id=1, source_target_pairs={{1,0},{2,1},{3,2},{4,3},{5,4},{6,5},{7,6},{8,7},{9,8},{10,9},{11,1... | collective-permute-start | bytes 49160 | tf_op jit(solution)/shard_map/ppermute | solution.py:25
  18.4 9.8 %copy-start = (s32[16]{0:T(128)S(1)}, s32[16]{0:T(128)}, u32[]{:S(2)}) copy-start(s32[16]{0:T(128)} %param.7) | copy-start | bytes 196
  18.4 21.1 %collective-permute-start.2 = (f32[32,1,4096]{2,0,1:T(8,128)S(1)}, f32[32,1,4096]{2,0,1:T(8,128)S(1)}, u32[]{:S(2)}, u32[]{:S(2)}) collective-permute-start(f32[32,1,4096]{2,0,1:T(8,128)S(1)} %get-tuple-element.41), channel_id=1, source_target_pairs={{0,1},{1,2},{2,3},{3,4},{4,5},{5,6},{6,7},{7,8},{8,9},{9,10},{10,1... | collective-permute-start | bytes 1572872 | tf_op jit(solution)/shard_map/ppermute | solution.py:23
  20.3 19.2 %collective-permute-start.3 = (f32[32,1,4096]{2,0,1:T(8,128)S(1)}, f32[32,1,4096]{2,0,1:T(8,128)S(1)}, u32[]{:S(2)}, u32[]{:S(2)}) collective-permute-start(f32[32,1,4096]{2,0,1:T(8,128)S(1)} %get-tuple-element.42), channel_id=1, source_target_pairs={{1,0},{2,1},{3,2},{4,3},{5,4},{6,5},{7,6},{8,7},{9,8},{10,9},{11,1... | collective-permute-start | bytes 1572872 | tf_op jit(solution)/shard_map/ppermute | solution.py:25
  28.8 182.7 %collective-permute-start.10 = (s32[1]{0:T(128)}, s32[1]{0:T(128)}, u32[]{:S(2)}, u32[]{:S(2)}) collective-permute-start(s32[1]{0:T(128)} %get-tuple-element.57), channel_id=1, source_target_pairs={{0,1},{1,2},{2,3},{3,4},{4,5},{5,6},{6,7},{7,8},{8,9},{9,10},{10,1... | collective-permute-start | bytes 20 | tf_op jit(solution)/shard_map/ppermute | solution.py:23
  31.4 180.1 %collective-permute-start.12 = (s32[1]{0:T(128)}, s32[1]{0:T(128)}, u32[]{:S(2)}, u32[]{:S(2)}) collective-permute-start(s32[1]{0:T(128)} %get-tuple-element.58), channel_id=1, source_target_pairs={{1,0},{2,1},{3,2},{4,3},{5,4},{6,5},{7,6},{8,7},{9,8},{10,9},{11,1... | collective-permute-start | bytes 20 | tf_op jit(solution)/shard_map/ppermute | solution.py:25
  40.8 14.7 %collective-permute-start.4 = (f32[32,1,4096]{2,0,1:T(8,128)S(1)}, f32[32,1,4096]{2,0,1:T(8,128)S(1)}, u32[]{:S(2)}, u32[]{:S(2)}) collective-permute-start(f32[32,1,4096]{2,0,1:T(8,128)S(1)} %get-tuple-element.35), channel_id=1, source_target_pairs={{0,1},{1,2},{2,3},{3,4},{4,5},{5,6},{6,7},{7,8},{8,9},{9,10},{10,1... | collective-permute-start | bytes 1572872 | tf_op jit(solution)/shard_map/ppermute | solution.py:23
  42.7 14.5 %collective-permute-start.5 = (f32[32,1,4096]{2,0,1:T(8,128)S(1)}, f32[32,1,4096]{2,0,1:T(8,128)S(1)}, u32[]{:S(2)}, u32[]{:S(2)}) collective-permute-start(f32[32,1,4096]{2,0,1:T(8,128)S(1)} %get-tuple-element.36), channel_id=1, source_target_pairs={{1,0},{2,1},{3,2},{4,3},{5,4},{6,5},{7,6},{8,7},{9,8},{10,9},{11,1... | collective-permute-start | bytes 1572872 | tf_op jit(solution)/shard_map/ppermute | solution.py:25
  58.4 14.9 %collective-permute-start.6 = (f32[32,1,4096]{2,0,1:T(8,128)S(1)}, f32[32,1,4096]{2,0,1:T(8,128)S(1)}, u32[]{:S(2)}, u32[]{:S(2)}) collective-permute-start(f32[32,1,4096]{2,0,1:T(8,128)S(1)} %get-tuple-element.29), channel_id=1, source_target_pairs={{0,1},{1,2},{2,3},{3,4},{4,5},{5,6},{6,7},{7,8},{8,9},{9,10},{10,1... | collective-permute-start | bytes 1572872 | tf_op jit(solution)/shard_map/ppermute | solution.py:23
  60.4 14.7 %collective-permute-start.7 = (f32[32,1,4096]{2,0,1:T(8,128)S(1)}, f32[32,1,4096]{2,0,1:T(8,128)S(1)}, u32[]{:S(2)}, u32[]{:S(2)}) collective-permute-start(f32[32,1,4096]{2,0,1:T(8,128)S(1)} %get-tuple-element.30), channel_id=1, source_target_pairs={{1,0},{2,1},{3,2},{4,3},{5,4},{6,5},{7,6},{8,7},{9,8},{10,9},{11,1... | collective-permute-start | bytes 1572872 | tf_op jit(solution)/shard_map/ppermute | solution.py:25
  76.3 14.9 %collective-permute-start.8 = (f32[32,1,4096]{2,0,1:T(8,128)S(1)}, f32[32,1,4096]{2,0,1:T(8,128)S(1)}, u32[]{:S(2)}, u32[]{:S(2)}) collective-permute-start(f32[32,1,4096]{2,0,1:T(8,128)S(1)} %get-tuple-element.19), channel_id=1, source_target_pairs={{0,1},{1,2},{2,3},{3,4},{4,5},{5,6},{6,7},{7,8},{8,9},{9,10},{10,1... | collective-permute-start | bytes 1572872 | tf_op jit(solution)/shard_map/ppermute | solution.py:23
  78.2 14.7 %collective-permute-start.9 = (f32[32,1,4096]{2,0,1:T(8,128)S(1)}, f32[32,1,4096]{2,0,1:T(8,128)S(1)}, u32[]{:S(2)}, u32[]{:S(2)}) collective-permute-start(f32[32,1,4096]{2,0,1:T(8,128)S(1)} %get-tuple-element.20), channel_id=1, source_target_pairs={{1,0},{2,1},{3,2},{4,3},{5,4},{6,5},{7,6},{8,7},{9,8},{10,9},{11,1... | collective-permute-start | bytes 1572872 | tf_op jit(solution)/shard_map/ppermute | solution.py:25
  201.7 11.1 %collective-permute-start.11 = (f32[1,1024]{1,0:T(1,128)S(1)}, f32[1,1024]{1,0:T(1,128)S(1)}, u32[]{:S(2)}, u32[]{:S(2)}) collective-permute-start(f32[1,1024]{1,0:T(1,128)S(1)} %get-tuple-element.45), channel_id=1, source_target_pairs={{0,1},{1,2},{2,3},{3,4},{4,5},{5,6},{6,7},{7,8},{8,9},{9,10},{10,1... | collective-permute-start | bytes 12296 | tf_op jit(solution)/shard_map/ppermute | solution.py:23
  203.6 9.2 %collective-permute-start.13 = (f32[1,1024]{1,0:T(1,128)S(1)}, f32[1,1024]{1,0:T(1,128)S(1)}, u32[]{:S(2)}, u32[]{:S(2)}) collective-permute-start(f32[1,1024]{1,0:T(1,128)S(1)} %get-tuple-element.46), channel_id=1, source_target_pairs={{1,0},{2,1},{3,2},{4,3},{5,4},{6,5},{7,6},{8,7},{9,8},{10,9},{11,1... | collective-permute-start | bytes 12296 | tf_op jit(solution)/shard_map/ppermute | solution.py:25
where the time goes:
time: 305 us
  blocking collectives  103 us (34%)
  other arithmetic  92.6 us (30%)
  starting transfers between devices  73.9 us (24%)
  waiting for transfers between devices  19.7 us (6%)
  local copies, waits for them, and re-layouts  10.2 us (3%)
  matrix products  3.89 us (1%)
    psum x1, blocking collectives, root_means(): total_sq = lax.psum(local_sq, 'slab')  103 us
    ppermute x7, starting transfers between devices, with_halo(): lax.ppermute(head, axis, [((i + 1) % count, i) for i in range(ends)])  60.4 us
    another operation x4, other arithmetic, factor(): return jnp.linalg.cholesky(gram_sum.reshape(block_count, width, width))  47.1 us
    another operation x2, other arithmetic, local(): lax.linalg.triangular_solve(lower_fac, blocks, left_side=True, lower=True)  39.4 us
    ppermute x7, waiting for transfers between devices, with_halo(): lax.ppermute(tail, axis, [(i, (i + 1) % count) for i in range(ends)])  14.4 us
    ppermute x7, starting transfers between devices, with_halo(): lax.ppermute(tail, axis, [(i, (i + 1) % count) for i in range(ends)])  13.4 us
  transfers between devices with their start and end apart: 14, of which 6 were waited for; matrix products, arithmetic and copies ran while one was open for 5% of the time, Pallas kernels for 0%

commit v1 on v0

v1 whole, which is shorter than its diff:
```python
import functools

import jax
import jax.numpy as jnp
from jax import lax
from jax.experimental import pallas as pl
from jax.experimental.pallas import tpu as pltpu
from jax.sharding import PartitionSpec as P

K = 32
BLKR = 512
NX = 256
NY = 16
PLANE = NX * NY
SWEEPS = 4
NMAT = 8
GROUP = 8
GROUPS = K // GROUP
BLOCKS = 16
PLANES = 2
CELLS = 1024 * PLANE

WEIGHT = 2.0 / 3.0
EPS = 1e-06
LIFT = 2.0**20


def reduce_groups(n):
    return ((1, 8), (128, 4), (8, 16)) if n == 512 else ((1, n),)


def kernel(
    n, sv, mat, table, ids, out, coarse,
    vec, halo, coef, cond, cond_out, cond_in, id_out, id_in,
    edge_out, edge_in, aug, rows, halves, sums, sums_in,
    load_sem, send_sem, recv_sem, small_send, small_recv, ar_send, ar_recv,
):
    me = lax.axis_index("slab")
    right, left = lax.rem(me + 1, n), lax.rem(me + n - 1, n)
    sides = (left, right)
    steps = reduce_groups(n)

    def partner(step, d):
        stride, size = steps[step]
        pos = lax.rem(lax.div(me, stride), size)
        return me + (lax.rem(pos + d, size) - pos) * stride

    def remote(src, dst, ssem, rsem, dev):
        return pltpu.make_async_remote_copy(
            src_ref=src, dst_ref=dst, send_sem=ssem, recv_sem=rsem,
            device_id=(dev,), device_id_type=pl.DeviceIdType.MESH,
        )

    barrier = pltpu.get_barrier_semaphore()
    count = 0
    targets = [left, right]
    for step, (_, size) in enumerate(steps):
        targets += [partner(step, d) for d in range(1, size)]
    for dev in targets:
        pl.semaphore_signal(barrier, inc=1, device_id=(dev,), device_id_type=pl.DeviceIdType.MESH)
        count += 1

    load = pltpu.make_async_copy(sv, vec.at[0], load_sem)
    load.start()

    for z in range(PLANES):
        for y in range(NY):
            cols = slice(y * NX, (y + 1) * NX)
            m = jnp.broadcast_to(mat[z : z + 1, cols], (8, NX))
            k = jnp.zeros((8, NX), jnp.float32)
            for j in range(NMAT):
                k = jnp.where(m == j, table[j], k)
            cond[z, :, cols] = k
            cond_out[z, :, cols] = k[0:1]
    id_out[0] = jnp.full((8, 128), ids[0], jnp.int32)
    id_out[1] = jnp.full((8, 128), ids[BLOCKS - 1], jnp.int32)

    pl.semaphore_wait(barrier, count)
    load.wait()

    small = []
    for z in range(PLANES):
        small.append(remote(cond_out.at[z], cond_in.at[1 - z], small_send.at[z], small_recv.at[z], sides[z]))
        small.append(remote(id_out.at[z], id_in.at[1 - z], small_send.at[2 + z], small_recv.at[2 + z], sides[z]))
    for c in small:
        c.start()

    def plane_copy(s, q, z):
        lanes = pl.ds(pl.multiple_of(q * GROUP, GROUP), GROUP)
        return remote(
            vec.at[s, z, lanes], halo.at[s, 1 - z, lanes],
            send_sem.at[s, q, z], recv_sem.at[s, q, z], sides[z],
        )

    for q in range(GROUPS):
        for z in range(PLANES):
            plane_copy(0, q, z).start()

    for c in small:
        c.wait_recv()

    has_below = (me > 0).astype(jnp.float32)
    has_above = (me < n - 1).astype(jnp.float32)
    xpos = lax.broadcasted_iota(jnp.int32, (8, NX), 1)
    west_ok, east_ok = xpos > 0, xpos < NX - 1

    def face(k, other):
        return 2.0 * k * other / (k + other)

    for z in range(PLANES):
        for y in range(NY):
            cols = slice(y * NX, (y + 1) * NX)
            k = cond[z, :, cols]
            zero = jnp.zeros_like(k)
            fw = face(k, pltpu.roll(k, 1, axis=1))
            fe = face(k, pltpu.roll(k, NX - 1, axis=1))
            fs = face(k, cond[z, :, (y - 1) * NX : y * NX]) if y > 0 else k
            fn = face(k, cond[z, :, (y + 1) * NX : (y + 2) * NX]) if y < NY - 1 else k
            below = cond[0, :, cols] if z == 1 else jnp.broadcast_to(cond_in[0, :, cols], (8, NX))
            above = cond[1, :, cols] if z == 0 else jnp.broadcast_to(cond_in[1, :, cols], (8, NX))
            fd, fu = face(k, below), face(k, above)
            hd = has_below if z == 0 else 1.0
            hu = has_above if z == 1 else 1.0
            dsum = (
                jnp.where(west_ok, fw, k) + jnp.where(east_ok, fe, k) + fs + fn
                + (hd * fd + (1.0 - hd) * k) + (hu * fu + (1.0 - hu) * k)
            )
            scale = WEIGHT / dsum
            coef[z, 0, :, cols] = jnp.where(west_ok, fw * scale, zero)
            coef[z, 1, :, cols] = jnp.where(east_ok, fe * scale, zero)
            coef[z, 2, :, cols] = fs * scale
            coef[z, 3, :, cols] = fn * scale
            coef[z, 4, :, cols] = fd * scale * hd
            coef[z, 5, :, cols] = fu * scale * hu

    def sweep(t, carry):
        s, q = lax.div(t, GROUPS), lax.rem(t, GROUPS)
        lanes = pl.ds(pl.multiple_of(q * GROUP, GROUP), GROUP)
        for z in range(PLANES):
            plane_copy(s, q, z).wait_recv()
        for z in range(PLANES):
            for y in range(NY):
                cols = slice(y * NX, (y + 1) * NX)
                c = vec[s, z, lanes, cols]
                acc = c * (1.0 - WEIGHT)
                acc += coef[z, 0, :, cols] * pltpu.roll(c, 1, axis=1)
                acc += coef[z, 1, :, cols] * pltpu.roll(c, NX - 1, axis=1)
                if y > 0:
                    acc += coef[z, 2, :, cols] * vec[s, z, lanes, (y - 1) * NX : y * NX]
                if y < NY - 1:
                    acc += coef[z, 3, :, cols] * vec[s, z, lanes, (y + 1) * NX : (y + 2) * NX]
                below = vec[s, 0, lanes, cols] if z == 1 else halo[s, 0, lanes, cols]
                above = vec[s, 1, lanes, cols] if z == 0 else halo[s, 1, lanes, cols]
                acc += coef[z, 4, :, cols] * below
                acc += coef[z, 5, :, cols] * above
                vec[s + 1, z, lanes, cols] = acc

            @pl.when(s < SWEEPS - 1)
            def _():
                plane_copy(s + 1, q, z).start()

        return carry

    lax.fori_loop(0, SWEEPS * GROUPS, sweep, 0)

    nt = (((1,), (1,)), ((), ()))
    dot = functools.partial(lax.dot_general, preferred_element_type=jnp.float32)
    local = []
    for b in range(BLOCKS):
        z, c = divmod(b, PLANE // BLKR)
        v = vec[SWEEPS, z, :, c * BLKR : (c + 1) * BLKR] * LIFT
        hi = v.astype(jnp.bfloat16)
        lo = (v - hi.astype(jnp.float32)).astype(jnp.bfloat16)
        halves[b, 0:K] = hi
        halves[b, K : 2 * K] = lo
        g = dot(hi, hi, nt) + dot(hi, lo, nt) + dot(lo, hi, nt)
        local.append(g * (1.0 / BLKR))

    same = [None] + [(ids[b] == ids[b - 1]).astype(jnp.float32) for b in range(1, BLOCKS)]
    run = [local[0]]
    for b in range(1, BLOCKS):
        run.append(local[b] + same[b] * run[b - 1])
    for b in range(BLOCKS - 2, -1, -1):
        run[b] = run[b] + same[b + 1] * (run[b + 1] - run[b])
    edge_out[0] = run[0]
    edge_out[1] = run[BLOCKS - 1]
    edges = [remote(edge_out.at[z], edge_in.at[1 - z], small_send.at[4 + z], small_recv.at[4 + z], sides[z]) for z in range(PLANES)]
    for c in edges:
        c.start()

    total = local[0]
    for b in range(1, BLOCKS):
        total = total + local[b]
    i_pos = lax.broadcasted_iota(jnp.int32, (K, K), 0)
    j_pos = lax.broadcasted_iota(jnp.int32, (K, K), 1)
    diag = jnp.sum(jnp.where(i_pos == j_pos, total, 0.0), axis=0, keepdims=True)
    diag = jnp.concatenate([diag, jnp.zeros((1, 128 - K), jnp.float32)], axis=1)
    sums[0] = jnp.broadcast_to(diag, (8, 128))

    slot0 = [sum(size - 1 for _, size in steps[:step]) for step in range(len(steps))]

    def reduce_copy(step, d):
        slot = slot0[step] + d - 1
        return remote(sums.at[step], sums_in.at[slot], ar_send.at[slot], ar_recv.at[slot], partner(step, d))

    def reduce_send(step):
        for d in range(1, steps[step][1]):
            reduce_copy(step, d).start()

    def reduce_recv(step):
        tot = sums[step]
        for d in range(1, steps[step][1]):
            reduce_copy(step, d).wait_recv()
            tot = tot + sums_in[slot0[step] + d - 1]
        sums[step + 1] = tot

    reduce_send(0)

    for c in edges:
        c.wait_recv()
    pad = jnp.zeros((K, 2 * K), jnp.float32)
    end = jnp.zeros((K, K), jnp.float32)
    for b in range(BLOCKS):
        from_left = jnp.where(id_in[0, 0:1, 0:K] == ids[b], 1.0, 0.0) * has_below
        from_right = jnp.where(id_in[1, 0:1, 0:K] == ids[b], 1.0, 0.0) * has_above
        g = run[b] + from_left * edge_in[0] + from_right * edge_in[1]
        aug[pl.ds(b, K, stride=BLOCKS), :] = jnp.concatenate([pad, g, end], axis=1)

    lane = lax.broadcasted_iota(jnp.int32, (BLOCKS, 128), 1)
    r = [
        aug[i * BLOCKS : (i + 1) * BLOCKS, :] + jnp.where((lane == i) | (lane == K + i), 1.0, 0.0)
        for i in range(K)
    ]
    done = 0
    for k in range(K):
        d = jnp.broadcast_to(r[k][:, 2 * K + k : 2 * K + k + 1], (BLOCKS, 128))
        scaled = r[k] / d
        for i in range(k + 1, K):
            r[i] = r[i] - jnp.broadcast_to(r[k][:, 2 * K + i : 2 * K + i + 1], (BLOCKS, 128)) * scaled
        keep = (lane < 2 * K) | (lane >= 2 * K + k)
        rows[k * BLOCKS : (k + 1) * BLOCKS, :] = jnp.where(keep, r[k] * lax.rsqrt(d), 0.0)
        if k % 8 == 7 and done < len(steps) - 1:
            reduce_recv(done)
            done += 1
            reduce_send(done)

    for b in range(BLOCKS):
        z, c = divmod(b, PLANE // BLKR)
        w = rows[pl.ds(b, K, stride=BLOCKS), :][:, 0 : 2 * K]
        hi = w.astype(jnp.bfloat16)
        lo = (w - hi.astype(jnp.float32)).astype(jnp.bfloat16)
        nn = (((1,), (0,)), ((), ()))
        x = halves[b]
        out[z, :, c * BLKR : (c + 1) * BLKR] = dot(hi, x, nn) + dot(lo, x, nn)

    while done < len(steps):
        reduce_recv(done)
        done += 1
        if done < len(steps):
            reduce_send(done)
    mean_sq = sums[len(steps)][0:1, 0:K] * (BLKR / CELLS)
    inv = lax.rsqrt(mean_sq + EPS * LIFT * LIFT)
    for b in range(BLOCKS):
        coarse[b] = rows[pl.ds(b, K, stride=BLOCKS), :][:, 2 * K : 3 * K] * inv

    for c in small + edges:
        c.wait_send()
    for step, (_, size) in enumerate(steps):
        for d in range(1, size):
            reduce_copy(step, d).wait_send()

    def drain(t, carry):
        for z in range(PLANES):
            plane_copy(lax.div(t, GROUPS), lax.rem(t, GROUPS), z).wait_send()
        return carry

    lax.fori_loop(0, SWEEPS * GROUPS, drain, 0)


def local(n, start_vectors, materials, conduct_table, aggregate_ids):
    f32 = jnp.float32
    steps = reduce_groups(n)
    slots = sum(size - 1 for _, size in steps)
    vmem, smem = pl.BlockSpec(memory_space=pltpu.VMEM), pl.BlockSpec(memory_space=pltpu.SMEM)
    out, coarse = pl.pallas_call(
        functools.partial(kernel, n),
        out_shape=(
            jax.ShapeDtypeStruct((PLANES, K, PLANE), f32),
            jax.ShapeDtypeStruct((BLOCKS, K, K), f32),
        ),
        in_specs=[pl.BlockSpec(memory_space=pl.ANY), vmem, smem, smem],
        out_specs=(vmem, vmem),
        scratch_shapes=[
            pltpu.VMEM((SWEEPS + 1, PLANES, K, PLANE), f32),
            pltpu.VMEM((SWEEPS, 2, K, PLANE), f32),
            pltpu.VMEM((PLANES, 6, 8, PLANE), f32),
            pltpu.VMEM((PLANES, 8, PLANE), f32),
            pltpu.VMEM((PLANES, 1, PLANE), f32),
            pltpu.VMEM((2, 1, PLANE), f32),
            pltpu.VMEM((2, 8, 128), jnp.int32),
            pltpu.VMEM((2, 8, 128), jnp.int32),
            pltpu.VMEM((2, K, K), f32),
            pltpu.VMEM((2, K, K), f32),
            pltpu.VMEM((K * BLOCKS, 128), f32),
            pltpu.VMEM((K * BLOCKS, 128), f32),
            pltpu.VMEM((BLOCKS, 2 * K, BLKR), jnp.bfloat16),
            pltpu.VMEM((len(steps) + 1, 8, 128), f32),
            pltpu.VMEM((slots, 8, 128), f32),
            pltpu.SemaphoreType.DMA,
            pltpu.SemaphoreType.DMA((SWEEPS, GROUPS, PLANES)),
            pltpu.SemaphoreType.DMA((SWEEPS, GROUPS, PLANES)),
            pltpu.SemaphoreType.DMA((6,)),
            pltpu.SemaphoreType.DMA((6,)),
            pltpu.SemaphoreType.DMA((slots,)),
            pltpu.SemaphoreType.DMA((slots,)),
        ],
        compiler_params=pltpu.CompilerParams(
            collective_id=0, has_side_effects=True, vmem_limit_bytes=40 * 2**20
        ),
        name="adaptive_setup",
    )(jnp.transpose(start_vectors, (1, 0, 2)), materials, conduct_table, aggregate_ids)
    return jnp.transpose(out, (1, 0, 2)), coarse


def solution(mesh):
    n = mesh.shape["slab"]
    return jax.shard_map(
        functools.partial(local, n),
        mesh=mesh,
        in_specs=(P(None, "slab", None), P("slab", None), P(), P("slab")),
        out_specs=(P(None, "slab", None), P("slab", None, None)),
        check_vma=False,
    )
```

time: 305 us -> 66 us (0.22)
  blocking collectives: 103 us -> 0 us
  other arithmetic: 92.6 us -> 0 us
  starting transfers between devices: 73.9 us -> 0 us
  Pallas kernels: 0 us -> 60.2 us
  waiting for transfers between devices: 19.7 us -> 0 us
  local copies, waits for them, and re-layouts: 10.2 us -> 4.98 us
  matrix products: 3.89 us -> 0 us
    psum x1 -> x0, blocking collectives: 103 us -> none  [root_means(): total_sq = lax.psum(local_sq, 'slab')]
    another operation x6 -> x0, other arithmetic: 86.5 us -> none  [the longest x4 47.1 us: factor(): return jnp.linalg.cholesky(gram_sum.reshape(block_count, width, width))]
    ppermute x14 -> x0, starting transfers between devices: 73.9 us -> none  [the longest x7 60.4 us: with_halo(): lax.ppermute(head, axis, [((i + 1) % count, i) for i in range(ends)])]
    pallas_call x0 -> x1, Pallas kernels: none -> 60.2 us  [local(): pl.pallas_call(functools.partial(kernel, n), out_shape=(jax.ShapeDtypeStr...]
    ppermute x14 -> x0, waiting for transfers between devices: 19.7 us -> none  [the longest x7 14.4 us: with_halo(): lax.ppermute(tail, axis, [(i, (i + 1) % count) for i in range(ends)])]
    reshape x5 -> x0, local copies, waits for them, and re-layouts: 3.15 us -> none  [the longest x1 1.86 us: local(): prolongator = jnp.transpose(solved, (1, 0, 2)).reshape(vectors.shape)]
  transfers between devices with their start and end apart: 14 -> 0, of which waited for: 6 -> 0; matrix products, arithmetic and copies ran while one was open for 5% -> 0% of each run, Pallas kernels for 0% -> 0%
where the time goes in v1:
time: 66 us; the launch traced here: 65.9 us
  Pallas kernels  60.2 us (91%)
  local copies, waits for them, and re-layouts  4.98 us (8%)
  between operations  0.67 us (1%)
    pallas_call x1, Pallas kernels, local(): pl.pallas_call(functools.partial(kernel, n), out_shape=(jax.ShapeDtypeStr...  60.2 us
    unnamed x9, local copies, waits for them, and re-layouts  4.98 us

profile of v1, /device:TPU:8, one launch (start us, length us, event | category | flops | bytes accessed | tf_op | source)
XLA Modules:
  0.0 65.9 jit_solution(15158001864621397743)
XLA Ops:
  0.6 0.0 copy-start
  0.6 1.8 %copy.9 = f32[32,2,4096]{2,0,1:T(8,128)S(1)} copy(f32[32,2,4096]{2,1,0:T(2,128)} %param.4) | data formatting | bytes 2097152 | tf_op args[0]
  2.5 0.0 copy-start.1
  2.5 0.0 copy-start.2
  2.5 0.0 copy-done
  2.5 0.6 copy-done.1
  3.1 0.0 copy-done.2
  3.2 60.2 %adaptive_setup.1 = (f32[2,32,4096]{2,1,0:T(8,128)S(1)}, f32[16,32,32]{2,1,0:T(8,128)S(1)}) custom-call(f32[2,32,4096]{2,1,0:T(8,128)S(1)} %bitcast.4, s32[2,4096]{1,0:T(2,128)S(1)} %copy-done, f32[8]{0:T(128)S(1)} %copy-done.1, s32[16]{0:T(128)S(1)} %copy-done.2), custom_call_target="tpu_custom_call" | custom-call | tf_op jit(solution)/shard_map/adaptive_setup/pallas_call | solution.py:285
  63.4 1.8 %copy.7 = f32[32,2,4096]{2,1,0:T(2,128)} copy(f32[32,2,4096]{2,0,1:T(8,128)S(1)} %bitcast.5) | data formatting | bytes 2097152
  65.2 0.7 %copy.11 = f32[16,32,32]{2,1,0:T(8,128)} copy(f32[16,32,32]{2,1,0:T(8,128)S(1)} %get-tuple-element.11) | data formatting | bytes 131072
Async XLA Ops:
  0.6 1.9 %copy-start = (s32[2,4096]{1,0:T(2,128)S(1)}, s32[2,4096]{1,0:T(2,128)}, u32[]{:S(2)}) copy-start(s32[2,4096]{1,0:T(2,128)} %mat.1) | copy-start | bytes 98308
  2.5 0.7 copy-start.1
  2.5 0.7 %copy-start.2 = (s32[16]{0:T(128)S(1)}, s32[16]{0:T(128)}, u32[]{:S(2)}) copy-start(s32[16]{0:T(128)} %ids.1) | copy-start | bytes 196

commit v2 on v1

--- a/solution.py
+++ b/solution.py
@@ -25,25 +25,38 @@
 LIFT = 2.0**20
 
 
-def reduce_groups(n):
-    return ((1, 8), (128, 4), (8, 16)) if n == 512 else ((1, n),)
+CORE, X, Y, Z = (1, 2), (2, 4), (128, 4), (8, 16)
+STEPS = ((CORE,), (X, Y), (Z,))
+ENTRY = ((X, 1), (X, 3), (Y, 1), (Y, 3), (Z, 1), (Z, 15))
+TOKENS = (ENTRY, ((X, 1), (X, 2), (X, 3), (Z, 2), (Z, 14)), ((Z, 4), (Z, 12)))
+
+
+def peers(step):
+    found = [()]
+    for axis in step:
+        found = [f + ((axis, d),) for f in found for d in range(axis[1])]
+    return [tuple(move for move in f if move[1]) for f in found if any(d for _, d in f)]
 
 
 def kernel(
-    n, sv, mat, table, ids, out, coarse,
-    vec, halo, coef, cond, cond_out, cond_in, id_out, id_in,
-    edge_out, edge_in, aug, rows, halves, sums, sums_in,
-    load_sem, send_sem, recv_sem, small_send, small_recv, ar_send, ar_recv,
+    n, sv, mat_hbm, table_hbm, ids_hbm, out, coarse,
+    raw, mat, table, ids, vec, halo, coef, cond, cond_out, cond_in, id_out, id_in,
+    edge_out, edge_in, aug, rows, halves, squares, sums, sums_in,
+    load_sem, send_sem, recv_sem, small_send, small_recv, ar_send, ar_recv, token,
 ):
     me = lax.axis_index("slab")
     right, left = lax.rem(me + 1, n), lax.rem(me + n - 1, n)
     sides = (left, right)
-    steps = reduce_groups(n)
-
-    def partner(step, d):
-        stride, size = steps[step]
-        pos = lax.rem(lax.div(me, stride), size)
-        return me + (lax.rem(pos + d, size) - pos) * stride
+
+    def moved(moves):
+        dev = me
+        for (stride, size), d in moves:
+            pos = lax.rem(lax.div(me, stride), size)
+            dev = dev + (lax.rem(pos + d, size) - pos) * stride
+        return dev
+
+    def signal(sem, dev):
+        pl.semaphore_signal(sem, inc=1, device_id=(dev,), device_id_type=pl.DeviceIdType.MESH)
 
     def remote(src, dst, ssem, rsem, dev):
         return pltpu.make_async_remote_copy(
@@ -52,16 +65,24 @@
         )
 
     barrier = pltpu.get_barrier_semaphore()
-    count = 0
-    targets = [left, right]
-    for step, (_, size) in enumerate(steps):
-        targets += [partner(step, d) for d in range(1, size)]
-    for dev in targets:
-        pl.semaphore_signal(barrier, inc=1, device_id=(dev,), device_id_type=pl.DeviceIdType.MESH)
-        count += 1
-
-    load = pltpu.make_async_copy(sv, vec.at[0], load_sem)
-    load.start()
+    known = [left, right] + [moved((move,)) for move in ENTRY]
+    for dev in known:
+        signal(barrier, dev)
+
+    first = [
+        pltpu.make_async_copy(mat_hbm, mat, load_sem.at[0]),
+        pltpu.make_async_copy(table_hbm, table, load_sem.at[1]),
+        pltpu.make_async_copy(ids_hbm, ids, load_sem.at[2]),
+    ]
+    part = GROUP * PLANE // 128 * PLANES
+    loads = [
+        pltpu.make_async_copy(sv.at[pl.ds(q * part, part)], raw.at[pl.ds(q * part, part)], load_sem.at[3 + q])
+        for q in range(GROUPS)
+    ]
+    for c in first + loads:
+        c.start()
+    for c in first:
+        c.wait()
 
     for z in range(PLANES):
         for y in range(NY):
@@ -75,8 +96,15 @@
     id_out[0] = jnp.full((8, 128), ids[0], jnp.int32)
     id_out[1] = jnp.full((8, 128), ids[BLOCKS - 1], jnp.int32)
 
-    pl.semaphore_wait(barrier, count)
-    load.wait()
+    for q in range(GROUPS):
+        loads[q].wait()
+        for z in range(PLANES):
+            for t in range(PLANE // 128):
+                vec[0, z, q * GROUP : (q + 1) * GROUP, t * 128 : (t + 1) * 128] = raw[
+                    pl.ds(q * part + t * PLANES + z, GROUP, stride=PLANE // 128 * PLANES), :
+                ]
+
+    pl.semaphore_wait(barrier, len(known))
 
     small = []
     for z in range(PLANES):
@@ -95,6 +123,16 @@
     for q in range(GROUPS):
         for z in range(PLANES):
             plane_copy(0, q, z).start()
+
+    def pass_token(turn):
+        for i, move in enumerate(TOKENS[turn]):
+            signal(token.at[turn, i], moved((move,)))
+
+    def take_token(turn):
+        for i in range(len(TOKENS[turn])):
+            pl.semaphore_wait(token.at[turn, i], 1)
+
+    pass_token(0)
 
     for c in small:
         c.wait_recv()
@@ -138,6 +176,7 @@
         lanes = pl.ds(pl.multiple_of(q * GROUP, GROUP), GROUP)
         for z in range(PLANES):
             plane_copy(s, q, z).wait_recv()
+        square = jnp.zeros((GROUP, NX), jnp.float32)
         for z in range(PLANES):
             for y in range(NY):
                 cols = slice(y * NX, (y + 1) * NX)
@@ -154,14 +193,49 @@
                 acc += coef[z, 4, :, cols] * below
                 acc += coef[z, 5, :, cols] * above
                 vec[s + 1, z, lanes, cols] = acc
+                square += acc * acc
 
             @pl.when(s < SWEEPS - 1)
             def _():
                 plane_copy(s + 1, q, z).start()
 
+        squares[lanes, :] = square[:, 0:128] + square[:, 128:NX]
         return carry
 
-    lax.fori_loop(0, SWEEPS * GROUPS, sweep, 0)
+    lax.fori_loop(0, GROUPS, sweep, 0)
+    take_token(0)
+    pass_token(1)
+    lax.fori_loop(GROUPS, 2 * GROUPS, sweep, 0)
+    take_token(1)
+    pass_token(2)
+    lax.fori_loop(2 * GROUPS, SWEEPS * GROUPS, sweep, 0)
+    take_token(2)
+
+    i_pos = lax.broadcasted_iota(jnp.int32, (K, 128), 0)
+    j_pos = lax.broadcasted_iota(jnp.int32, (K, 128), 1)
+    each = jnp.sum(squares[...], axis=1, keepdims=True)
+    row = jnp.sum(jnp.where(i_pos == j_pos, each, 0.0), axis=0, keepdims=True)
+    sums[0] = jnp.broadcast_to(row, (8, 128))
+
+    groups = [peers(step) for step in STEPS]
+    slot0 = [sum(len(g) for g in groups[:step]) for step in range(len(STEPS))]
+
+    def reduce_copy(step, d):
+        slot = slot0[step] + d
+        return remote(sums.at[step], sums_in.at[slot], ar_send.at[slot], ar_recv.at[slot], moved(groups[step][d]))
+
+    def reduce_send(step):
+        for d in range(len(groups[step])):
+            reduce_copy(step, d).start()
+
+    def reduce_recv(step):
+        tot = sums[step]
+        for d in range(len(groups[step])):
+            reduce_copy(step, d).wait_recv()
+            tot = tot + sums_in[slot0[step] + d]
+        sums[step + 1] = tot
+
+    reduce_send(0)
 
     nt = (((1,), (1,)), ((), ()))
     dot = functools.partial(lax.dot_general, preferred_element_type=jnp.float32)
@@ -175,6 +249,9 @@
         halves[b, K : 2 * K] = lo
         g = dot(hi, hi, nt) + dot(hi, lo, nt) + dot(lo, hi, nt)
         local.append(g * (1.0 / BLKR))
+        if b == BLOCKS // 2 - 1:
+            reduce_recv(0)
+            reduce_send(1)
 
     same = [None] + [(ids[b] == ids[b - 1]).astype(jnp.float32) for b in range(1, BLOCKS)]
     run = [local[0]]
@@ -188,34 +265,6 @@
     for c in edges:
         c.start()
 
-    total = local[0]
-    for b in range(1, BLOCKS):
-        total = total + local[b]
-    i_pos = lax.broadcasted_iota(jnp.int32, (K, K), 0)
-    j_pos = lax.broadcasted_iota(jnp.int32, (K, K), 1)
-    diag = jnp.sum(jnp.where(i_pos == j_pos, total, 0.0), axis=0, keepdims=True)
-    diag = jnp.concatenate([diag, jnp.zeros((1, 128 - K), jnp.float32)], axis=1)
-    sums[0] = jnp.broadcast_to(diag, (8, 128))
-
-    slot0 = [sum(size - 1 for _, size in steps[:step]) for step in range(len(steps))]
-
-    def reduce_copy(step, d):
-        slot = slot0[step] + d - 1
-        return remote(sums.at[step], sums_in.at[slot], ar_send.at[slot], ar_recv.at[slot], partner(step, d))
-
-    def reduce_send(step):
-        for d in range(1, steps[step][1]):
-            reduce_copy(step, d).start()
-
-    def reduce_recv(step):
-        tot = sums[step]
-        for d in range(1, steps[step][1]):
-            reduce_copy(step, d).wait_recv()
-            tot = tot + sums_in[slot0[step] + d - 1]
-        sums[step + 1] = tot
-
-    reduce_send(0)
-
     for c in edges:
         c.wait_recv()
     pad = jnp.zeros((K, 2 * K), jnp.float32)
@@ -226,12 +275,14 @@
         g = run[b] + from_left * edge_in[0] + from_right * edge_in[1]
         aug[pl.ds(b, K, stride=BLOCKS), :] = jnp.concatenate([pad, g, end], axis=1)
 
+    reduce_recv(1)
+    reduce_send(2)
+
     lane = lax.broadcasted_iota(jnp.int32, (BLOCKS, 128), 1)
     r = [
         aug[i * BLOCKS : (i + 1) * BLOCKS, :] + jnp.where((lane == i) | (lane == K + i), 1.0, 0.0)
         for i in range(K)
     ]
-    done = 0
     for k in range(K):
         d = jnp.broadcast_to(r[k][:, 2 * K + k : 2 * K + k + 1], (BLOCKS, 128))
         scaled = r[k] / d
@@ -239,10 +290,6 @@
             r[i] = r[i] - jnp.broadcast_to(r[k][:, 2 * K + i : 2 * K + i + 1], (BLOCKS, 128)) * scaled
         keep = (lane < 2 * K) | (lane >= 2 * K + k)
         rows[k * BLOCKS : (k + 1) * BLOCKS, :] = jnp.where(keep, r[k] * lax.rsqrt(d), 0.0)
-        if k % 8 == 7 and done < len(steps) - 1:
-            reduce_recv(done)
-            done += 1
-            reduce_send(done)
 
     for b in range(BLOCKS):
         z, c = divmod(b, PLANE // BLKR)
@@ -251,22 +298,20 @@
         lo = (w - hi.astype(jnp.float32)).astype(jnp.bfloat16)
         nn = (((1,), (0,)), ((), ()))
         x = halves[b]
-        out[z, :, c * BLKR : (c + 1) * BLKR] = dot(hi, x, nn) + dot(lo, x, nn)
-
-    while done < len(steps):
-        reduce_recv(done)
-        done += 1
-        if done < len(steps):
-            reduce_send(done)
-    mean_sq = sums[len(steps)][0:1, 0:K] * (BLKR / CELLS)
-    inv = lax.rsqrt(mean_sq + EPS * LIFT * LIFT)
+        p = dot(hi, x, nn) + dot(lo, x, nn)
+        for t in range(BLKR // 128):
+            out[pl.ds((c * (BLKR // 128) + t) * PLANES + z, K, stride=PLANE // 128 * PLANES), :] = p[:, t * 128 : (t + 1) * 128]
+
+    reduce_recv(2)
+    mean_sq = sums[len(STEPS)][0:1, 0:K] * (1.0 / CELLS)
+    inv = lax.rsqrt(mean_sq + EPS) * (1.0 / LIFT)
     for b in range(BLOCKS):
         coarse[b] = rows[pl.ds(b, K, stride=BLOCKS), :][:, 2 * K : 3 * K] * inv
 
     for c in small + edges:
         c.wait_send()
-    for step, (_, size) in enumerate(steps):
-        for d in range(1, size):
+    for step in range(len(STEPS)):
+        for d in range(len(groups[step])):
             reduce_copy(step, d).wait_send()
 
     def drain(t, carry):
@@ -277,20 +322,28 @@
     lax.fori_loop(0, SWEEPS * GROUPS, drain, 0)
 
 
+def lines_of(vectors):
+    return jnp.transpose(vectors.reshape(K, PLANES, PLANE // 128, 128), (0, 2, 1, 3)).reshape(-1, 128)
+
+
 def local(n, start_vectors, materials, conduct_table, aggregate_ids):
     f32 = jnp.float32
-    steps = reduce_groups(n)
-    slots = sum(size - 1 for _, size in steps)
-    vmem, smem = pl.BlockSpec(memory_space=pltpu.VMEM), pl.BlockSpec(memory_space=pltpu.SMEM)
+    slots = sum(len(peers(step)) for step in STEPS)
+    lines = K * PLANES * PLANE // 128
+    vmem, anywhere = pl.BlockSpec(memory_space=pltpu.VMEM), pl.BlockSpec(memory_space=pl.ANY)
     out, coarse = pl.pallas_call(
         functools.partial(kernel, n),
         out_shape=(
-            jax.ShapeDtypeStruct((PLANES, K, PLANE), f32),
+            jax.ShapeDtypeStruct((lines, 128), f32),
             jax.ShapeDtypeStruct((BLOCKS, K, K), f32),
         ),
-        in_specs=[pl.BlockSpec(memory_space=pl.ANY), vmem, smem, smem],
+        in_specs=[anywhere] * 4,
         out_specs=(vmem, vmem),
         scratch_shapes=[
+            pltpu.VMEM((lines, 128), f32),
+            pltpu.VMEM((PLANES, PLANE), jnp.int32),
+            pltpu.SMEM((NMAT,), f32),
+            pltpu.SMEM((BLOCKS,), jnp.int32),
             pltpu.VMEM((SWEEPS + 1, PLANES, K, PLANE), f32),
             pltpu.VMEM((SWEEPS, 2, K, PLANE), f32),
             pltpu.VMEM((PLANES, 6, 8, PLANE), f32),
@@ -304,22 +357,25 @@
             pltpu.VMEM((K * BLOCKS, 128), f32),
             pltpu.VMEM((K * BLOCKS, 128), f32),
             pltpu.VMEM((BLOCKS, 2 * K, BLKR), jnp.bfloat16),
-            pltpu.VMEM((len(steps) + 1, 8, 128), f32),
+            pltpu.VMEM((K, 128), f32),
+            pltpu.VMEM((len(STEPS) + 1, 8, 128), f32),
             pltpu.VMEM((slots, 8, 128), f32),
-            pltpu.SemaphoreType.DMA,
+            pltpu.SemaphoreType.DMA((3 + GROUPS,)),
             pltpu.SemaphoreType.DMA((SWEEPS, GROUPS, PLANES)),
             pltpu.SemaphoreType.DMA((SWEEPS, GROUPS, PLANES)),
             pltpu.SemaphoreType.DMA((6,)),
             pltpu.SemaphoreType.DMA((6,)),
             pltpu.SemaphoreType.DMA((slots,)),
             pltpu.SemaphoreType.DMA((slots,)),
+            pltpu.SemaphoreType.REGULAR((len(TOKENS), len(ENTRY))),
         ],
         compiler_params=pltpu.CompilerParams(
             collective_id=0, has_side_effects=True, vmem_limit_bytes=40 * 2**20
         ),
         name="adaptive_setup",
-    )(jnp.transpose(start_vectors, (1, 0, 2)), materials, conduct_table, aggregate_ids)
-    return jnp.transpose(out, (1, 0, 2)), coarse
+    )(lines_of(start_vectors), materials, conduct_table, aggregate_ids)
+    out = jnp.transpose(out.reshape(K, PLANE // 128, PLANES, 128), (0, 2, 1, 3)).reshape(K, PLANES, PLANE)
+    return out, coarse
 
 
 def solution(mesh):

time: 66 us -> 60 us (0.909)
  the two profiles are of different devices: /device:TPU:8 before, /device:TPU:2 now
where the time goes in v2:
time: 60 us; the launch traced here: 59.7 us
  Pallas kernels  54.8 us (91%)
  local copies, waits for them, and re-layouts  4.31 us (7%)
  between operations  0.66 us (1%)
    pallas_call x1, Pallas kernels, local(): pl.pallas_call(functools.partial(kernel, n), out_shape=(jax.ShapeDtypeStr...  54.8 us
    unnamed x10, local copies, waits for them, and re-layouts  4.31 us

profile of v2, /device:TPU:2, one launch (start us, length us, event | category | flops | bytes accessed | tf_op | source)
XLA Modules:
  0.0 59.7 jit_solution(14280866267379014604)
XLA Ops:
  0.6 0.0 copy-start.3
  0.6 0.0 copy-start.2
  0.7 0.6 %copy-done.3 = s32[16]{0:T(128)S(1)} copy-done((s32[16]{0:T(128)S(1)}, s32[16]{0:T(128)}, u32[]{:S(2)}) %copy-start.3) | copy-done | bytes 88
  1.3 0.0 copy-done.2
  1.3 0.0 copy-start
  1.3 1.2 %copy-done = f32[32,2,4096]{2,1,0:T(2,128)S(1)} copy-done((f32[32,2,4096]{2,1,0:T(2,128)S(1)}, f32[32,2,4096]{2,1,0:T(2,128)}, u32[]{:S(2)}) %copy-start) | copy-done | bytes 1048600
  2.5 0.0 copy-start.1
  2.5 0.8 %copy-done.1 = s32[2,4096]{1,0:T(2,128)S(1)} copy-done((s32[2,4096]{1,0:T(2,128)S(1)}, s32[2,4096]{1,0:T(2,128)}, u32[]{:S(2)}) %copy-start.1) | copy-done | bytes 32792
  3.3 54.8 %adaptive_setup.1 = (f32[2048,128]{1,0:T(8,128)S(1)}, f32[16,32,32]{2,1,0:T(8,128)S(1)}) custom-call(f32[2048,128]{1,0:T(8,128)S(1)} %bitcast.10, s32[2,4096]{1,0:T(2,128)S(1)} %copy-done.1, f32[8]{0:T(128)S(1)} %copy-done.2, s32[16]{0:T(128)S(1)} %copy-done.3), custom_call_target="tpu_custom_call" | custom-call | tf_op jit(solution)/shard_map/adaptive_setup/pallas_call | solution.py:334
  58.1 1.0 %copy.10 = f32[32,2,4096]{2,1,0:T(2,128)} copy(f32[32,2,4096]{2,1,0:T(2,128)S(1)} %bitcast.11) | data formatting | bytes 2097152
  59.0 0.7 %copy.11 = f32[16,32,32]{2,1,0:T(8,128)} copy(f32[16,32,32]{2,1,0:T(8,128)S(1)} %get-tuple-element.9) | data formatting | bytes 131072
Async XLA Ops:
  0.6 0.7 %copy-start.3 = (s32[16]{0:T(128)S(1)}, s32[16]{0:T(128)}, u32[]{:S(2)}) copy-start(s32[16]{0:T(128)} %ids_hbm.1) | copy-start | bytes 196
  0.6 0.7 %copy-start.2 = (f32[8]{0:T(128)S(1)}, f32[8]{0:T(128)}, u32[]{:S(2)}) copy-start(f32[8]{0:T(128)} %table_hbm.1) | copy-start | bytes 100
  1.3 1.2 %copy-start = (f32[32,2,4096]{2,1,0:T(2,128)S(1)}, f32[32,2,4096]{2,1,0:T(2,128)}, u32[]{:S(2)}) copy-start(f32[32,2,4096]{2,1,0:T(2,128)} %param.4) | copy-start | bytes 3145732
  2.5 0.8 %copy-start.1 = (s32[2,4096]{1,0:T(2,128)S(1)}, s32[2,4096]{1,0:T(2,128)}, u32[]{:S(2)}) copy-start(s32[2,4096]{1,0:T(2,128)} %mat_hbm.1) | copy-start | bytes 98308

commit v3 on v2

--- a/solution.py
+++ b/solution.py
@@ -39,14 +39,16 @@
 
 
 def kernel(
-    n, sv, mat_hbm, table_hbm, ids_hbm, out, coarse,
+    n, sv, mat_hbm, table_hbm, ids_hbm, out, rows, total,
     raw, mat, table, ids, vec, halo, coef, cond, cond_out, cond_in, id_out, id_in,
-    edge_out, edge_in, aug, rows, halves, squares, sums, sums_in,
+    edge_out, edge_in, aug, halves, squares, sums, sums_in,
     load_sem, send_sem, recv_sem, small_send, small_recv, ar_send, ar_recv, token,
 ):
     me = lax.axis_index("slab")
     right, left = lax.rem(me + 1, n), lax.rem(me + n - 1, n)
     sides = (left, right)
+    to_ok = (me > 0, me < n - 1)
+    from_ok = (me < n - 1, me > 0)
 
     def moved(moves):
         dev = me
@@ -65,9 +67,15 @@
         )
 
     barrier = pltpu.get_barrier_semaphore()
-    known = [left, right] + [moved((move,)) for move in ENTRY]
-    for dev in known:
-        signal(barrier, dev)
+    for move in ENTRY:
+        signal(barrier, moved((move,)))
+    for z in range(PLANES):
+
+        @pl.when(to_ok[z])
+        def _():
+            signal(barrier, sides[z])
+
+    entries = len(ENTRY) + to_ok[0].astype(jnp.int32) + to_ok[1].astype(jnp.int32)
 
     first = [
         pltpu.make_async_copy(mat_hbm, mat, load_sem.at[0]),
@@ -96,22 +104,31 @@
     id_out[0] = jnp.full((8, 128), ids[0], jnp.int32)
     id_out[1] = jnp.full((8, 128), ids[BLOCKS - 1], jnp.int32)
 
-    for q in range(GROUPS):
-        loads[q].wait()
-        for z in range(PLANES):
-            for t in range(PLANE // 128):
-                vec[0, z, q * GROUP : (q + 1) * GROUP, t * 128 : (t + 1) * 128] = raw[
-                    pl.ds(q * part + t * PLANES + z, GROUP, stride=PLANE // 128 * PLANES), :
-                ]
-
-    pl.semaphore_wait(barrier, len(known))
-
-    small = []
-    for z in range(PLANES):
-        small.append(remote(cond_out.at[z], cond_in.at[1 - z], small_send.at[z], small_recv.at[z], sides[z]))
-        small.append(remote(id_out.at[z], id_in.at[1 - z], small_send.at[2 + z], small_recv.at[2 + z], sides[z]))
-    for c in small:
-        c.start()
+    pl.semaphore_wait(barrier, entries)
+
+    def send(z, copy):
+        @pl.when(to_ok[z])
+        def _():
+            copy().start()
+
+    def sent(z, copy):
+        @pl.when(to_ok[z])
+        def _():
+            copy().wait_send()
+
+    def received(z, copy):
+        @pl.when(from_ok[z])
+        def _():
+            copy().wait_recv()
+
+
+    def small_copy(z, i):
+        src, dst = ((cond_out, cond_in), (id_out, id_in), (edge_out, edge_in))[i]
+        return remote(src.at[z], dst.at[1 - z], small_send.at[i, z], small_recv.at[i, z], sides[z])
+
+    for i in range(2):
+        for z in range(PLANES):
+            send(z, functools.partial(small_copy, z, i))
 
     def plane_copy(s, q, z):
         lanes = pl.ds(pl.multiple_of(q * GROUP, GROUP), GROUP)
@@ -121,8 +138,13 @@
         )
 
     for q in range(GROUPS):
-        for z in range(PLANES):
-            plane_copy(0, q, z).start()
+        loads[q].wait()
+        for z in range(PLANES):
+            for t in range(PLANE // 128):
+                vec[0, z, q * GROUP : (q + 1) * GROUP, t * 128 : (t + 1) * 128] = raw[
+                    pl.ds(q * part + t * PLANES + z, GROUP, stride=PLANE // 128 * PLANES), :
+                ]
+            send(z, functools.partial(plane_copy, 0, q, z))
 
     def pass_token(turn):
         for i, move in enumerate(TOKENS[turn]):
@@ -134,8 +156,25 @@
 
     pass_token(0)
 
-    for c in small:
-        c.wait_recv()
+    for z in range(PLANES):
+
+        @pl.when(jnp.logical_not(from_ok[z]))
+        def _():
+            cond_in[1 - z] = jnp.zeros((1, PLANE), jnp.float32)
+            id_in[1 - z] = jnp.zeros((8, 128), jnp.int32)
+            edge_in[1 - z] = jnp.zeros((K, K), jnp.float32)
+
+            def clear(t, carry):
+                s, q = lax.div(t, GROUPS), lax.rem(t, GROUPS)
+                lanes = pl.ds(pl.multiple_of(q * GROUP, GROUP), GROUP)
+                halo[s, 1 - z, lanes] = jnp.zeros((GROUP, PLANE), jnp.float32)
+                return carry
+
+            lax.fori_loop(0, SWEEPS * GROUPS, clear, 0)
+
+    for i in range(2):
+        for z in range(PLANES):
+            received(z, functools.partial(small_copy, z, i))
 
     has_below = (me > 0).astype(jnp.float32)
     has_above = (me < n - 1).astype(jnp.float32)
@@ -175,7 +214,7 @@
         s, q = lax.div(t, GROUPS), lax.rem(t, GROUPS)
         lanes = pl.ds(pl.multiple_of(q * GROUP, GROUP), GROUP)
         for z in range(PLANES):
-            plane_copy(s, q, z).wait_recv()
+            received(z, functools.partial(plane_copy, s, q, z))
         square = jnp.zeros((GROUP, NX), jnp.float32)
         for z in range(PLANES):
             for y in range(NY):
@@ -195,7 +234,7 @@
                 vec[s + 1, z, lanes, cols] = acc
                 square += acc * acc
 
-            @pl.when(s < SWEEPS - 1)
+            @pl.when((s < SWEEPS - 1) & to_ok[z])
             def _():
                 plane_copy(s + 1, q, z).start()
 
@@ -215,7 +254,7 @@
     j_pos = lax.broadcasted_iota(jnp.int32, (K, 128), 1)
     each = jnp.sum(squares[...], axis=1, keepdims=True)
     row = jnp.sum(jnp.where(i_pos == j_pos, each, 0.0), axis=0, keepdims=True)
-    sums[0] = jnp.broadcast_to(row, (8, 128))
+    sums[0] = row
 
     groups = [peers(step) for step in STEPS]
     slot0 = [sum(len(g) for g in groups[:step]) for step in range(len(STEPS))]
@@ -233,7 +272,7 @@
         for d in range(len(groups[step])):
             reduce_copy(step, d).wait_recv()
             tot = tot + sums_in[slot0[step] + d]
-        sums[step + 1] = tot
+        return tot
 
     reduce_send(0)
 
@@ -250,7 +289,7 @@
         g = dot(hi, hi, nt) + dot(hi, lo, nt) + dot(lo, hi, nt)
         local.append(g * (1.0 / BLKR))
         if b == BLOCKS // 2 - 1:
-            reduce_recv(0)
+            sums[1] = reduce_recv(0)
             reduce_send(1)
 
     same = [None] + [(ids[b] == ids[b - 1]).astype(jnp.float32) for b in range(1, BLOCKS)]
@@ -261,12 +300,11 @@
         run[b] = run[b] + same[b + 1] * (run[b + 1] - run[b])
     edge_out[0] = run[0]
     edge_out[1] = run[BLOCKS - 1]
-    edges = [remote(edge_out.at[z], edge_in.at[1 - z], small_send.at[4 + z], small_recv.at[4 + z], sides[z]) for z in range(PLANES)]
-    for c in edges:
-        c.start()
-
-    for c in edges:
-        c.wait_recv()
+    for z in range(PLANES):
+        send(z, functools.partial(small_copy, z, 2))
+
+    for z in range(PLANES):
+        received(z, functools.partial(small_copy, z, 2))
     pad = jnp.zeros((K, 2 * K), jnp.float32)
     end = jnp.zeros((K, K), jnp.float32)
     for b in range(BLOCKS):
@@ -275,7 +313,7 @@
         g = run[b] + from_left * edge_in[0] + from_right * edge_in[1]
         aug[pl.ds(b, K, stride=BLOCKS), :] = jnp.concatenate([pad, g, end], axis=1)
 
-    reduce_recv(1)
+    sums[2] = reduce_recv(1)
     reduce_send(2)
 
     lane = lax.broadcasted_iota(jnp.int32, (BLOCKS, 128), 1)
@@ -302,24 +340,37 @@
         for t in range(BLKR // 128):
             out[pl.ds((c * (BLKR // 128) + t) * PLANES + z, K, stride=PLANE // 128 * PLANES), :] = p[:, t * 128 : (t + 1) * 128]
 
-    reduce_recv(2)
-    mean_sq = sums[len(STEPS)][0:1, 0:K] * (1.0 / CELLS)
-    inv = lax.rsqrt(mean_sq + EPS) * (1.0 / LIFT)
-    for b in range(BLOCKS):
-        coarse[b] = rows[pl.ds(b, K, stride=BLOCKS), :][:, 2 * K : 3 * K] * inv
-
-    for c in small + edges:
-        c.wait_send()
+    total[...] = reduce_recv(2)
+
+    for i in range(3):
+        for z in range(PLANES):
+            sent(z, functools.partial(small_copy, z, i))
     for step in range(len(STEPS)):
         for d in range(len(groups[step])):
             reduce_copy(step, d).wait_send()
 
     def drain(t, carry):
         for z in range(PLANES):
-            plane_copy(lax.div(t, GROUPS), lax.rem(t, GROUPS), z).wait_send()
+            sent(z, functools.partial(plane_copy, lax.div(t, GROUPS), lax.rem(t, GROUPS), z))
         return carry
 
     lax.fori_loop(0, SWEEPS * GROUPS, drain, 0)
+
+
+def finish(found, rows_in, total_in, out, coarse, rows, total, scaled, sem):
+    large = pltpu.make_async_copy(found, out, sem.at[0])
+    parts = [pltpu.make_async_copy(rows_in, rows, sem.at[2]), pltpu.make_async_copy(total_in, total, sem.at[3])]
+    for c in parts + [large]:
+        c.start()
+    for c in parts:
+        c.wait()
+    inv = lax.rsqrt(total[0:1, 0:K] * (1.0 / CELLS) + EPS) * (1.0 / LIFT)
+    for b in range(BLOCKS):
+        scaled[b] = rows[pl.ds(b, K, stride=BLOCKS), :][:, 2 * K : 3 * K] * inv
+    small = pltpu.make_async_copy(scaled, coarse, sem.at[1])
+    small.start()
+    large.wait()
+    small.wait()
 
 
 def lines_of(vectors):
@@ -331,14 +382,15 @@
     slots = sum(len(peers(step)) for step in STEPS)
     lines = K * PLANES * PLANE // 128
     vmem, anywhere = pl.BlockSpec(memory_space=pltpu.VMEM), pl.BlockSpec(memory_space=pl.ANY)
-    out, coarse = pl.pallas_call(
+    found, rows, total = pl.pallas_call(
         functools.partial(kernel, n),
         out_shape=(
             jax.ShapeDtypeStruct((lines, 128), f32),
-            jax.ShapeDtypeStruct((BLOCKS, K, K), f32),
+            jax.ShapeDtypeStruct((K * BLOCKS, 128), f32),
+            jax.ShapeDtypeStruct((1, 128), f32),
         ),
         in_specs=[anywhere] * 4,
-        out_specs=(vmem, vmem),
+        out_specs=(vmem, vmem, vmem),
         scratch_shapes=[
             pltpu.VMEM((lines, 128), f32),
             pltpu.VMEM((PLANES, PLANE), jnp.int32),
@@ -355,25 +407,38 @@
             pltpu.VMEM((2, K, K), f32),
             pltpu.VMEM((2, K, K), f32),
             pltpu.VMEM((K * BLOCKS, 128), f32),
-            pltpu.VMEM((K * BLOCKS, 128), f32),
             pltpu.VMEM((BLOCKS, 2 * K, BLKR), jnp.bfloat16),
             pltpu.VMEM((K, 128), f32),
-            pltpu.VMEM((len(STEPS) + 1, 8, 128), f32),
-            pltpu.VMEM((slots, 8, 128), f32),
+            pltpu.VMEM((len(STEPS), 1, 128), f32),
+            pltpu.VMEM((slots, 1, 128), f32),
             pltpu.SemaphoreType.DMA((3 + GROUPS,)),
             pltpu.SemaphoreType.DMA((SWEEPS, GROUPS, PLANES)),
             pltpu.SemaphoreType.DMA((SWEEPS, GROUPS, PLANES)),
-            pltpu.SemaphoreType.DMA((6,)),
-            pltpu.SemaphoreType.DMA((6,)),
+            pltpu.SemaphoreType.DMA((3, PLANES)),
+            pltpu.SemaphoreType.DMA((3, PLANES)),
             pltpu.SemaphoreType.DMA((slots,)),
             pltpu.SemaphoreType.DMA((slots,)),
             pltpu.SemaphoreType.REGULAR((len(TOKENS), len(ENTRY))),
         ],
         compiler_params=pltpu.CompilerParams(
-            collective_id=0, has_side_effects=True, vmem_limit_bytes=40 * 2**20
+            collective_id=0, has_side_effects=True, vmem_limit_bytes=54840524
         ),
         name="adaptive_setup",
     )(lines_of(start_vectors), materials, conduct_table, aggregate_ids)
+    out, coarse = pl.pallas_call(
+        finish,
+        out_shape=(jax.ShapeDtypeStruct((lines, 128), f32), jax.ShapeDtypeStruct((BLOCKS, K, K), f32)),
+        in_specs=[anywhere] * 3,
+        out_specs=(anywhere, anywhere),
+        scratch_shapes=[
+            pltpu.VMEM((K * BLOCKS, 128), f32),
+            pltpu.VMEM((1, 128), f32),
+            pltpu.VMEM((BLOCKS, K, K), f32),
+            pltpu.SemaphoreType.DMA((4,)),
+        ],
+        compiler_params=pltpu.CompilerParams(vmem_limit_bytes=2 * 2**20),
+        name="adaptive_finish",
+    )(found, rows, total)
     out = jnp.transpose(out.reshape(K, PLANE // 128, PLANES, 128), (0, 2, 1, 3)).reshape(K, PLANES, PLANE)
     return out, coarse
 

time: 60 us -> 56.2 us (0.937)
  the two profiles are of different devices: /device:TPU:2 before, /device:TPU:32 now
where the time goes in v3:
time: 56.2 us; the launch traced here: 56 us
  Pallas kernels  53.9 us (96%)
  local copies, waits for them, and re-layouts  1.41 us (3%)
  between operations  0.66 us (1%)
    pallas_call x1, Pallas kernels, local(): pl.pallas_call(functools.partial(kernel, n), out_shape=(jax.ShapeDtypeStr...  52.8 us
    unnamed x6, local copies, waits for them, and re-layouts  1.41 us

profile of v3, /device:TPU:32, one launch (start us, length us, event | category | flops | bytes accessed | tf_op | source)
XLA Modules:
  0.0 56.0 jit_solution(17800851915527841362)
XLA Ops:
  0.6 0.0 copy-start.2
  0.6 0.0 copy-start.1
  0.7 0.6 %copy-done.2 = s32[16]{0:T(128)S(1)} copy-done((s32[16]{0:T(128)S(1)}, s32[16]{0:T(128)}, u32[]{:S(2)}) %copy-start.2) | copy-done | bytes 88
  1.3 0.0 copy-done.1
  1.3 0.0 copy-start
  1.3 0.8 %copy-done = s32[2,4096]{1,0:T(2,128)S(1)} copy-done((s32[2,4096]{1,0:T(2,128)S(1)}, s32[2,4096]{1,0:T(2,128)}, u32[]{:S(2)}) %copy-start) | copy-done | bytes 32792
  2.1 52.8 %adaptive_setup.1 = (f32[2048,128]{1,0:T(8,128)S(1)}, f32[512,128]{1,0:T(8,128)S(1)}, f32[1,128]{1,0:T(1,128)S(1)}) custom-call(f32[2048,128]{1,0:T(8,128)} %bitcast.10, s32[2,4096]{1,0:T(2,128)S(1)} %copy-done, f32[8]{0:T(128)S(1)} %copy-done.1, s32[16]{0:T(128)S(1)} %copy-done.2), custom_call_target="tpu_custom_call" | custom-call | tf_op jit(solution)/shard_map/adaptive_setup/pallas_call | solution.py:385
  54.9 1.1 %adaptive_finish.1 = (f32[2048,128]{1,0:T(8,128)}, f32[16,32,32]{2,1,0:T(8,128)}) custom-call(f32[2048,128]{1,0:T(8,128)S(1)} %get-tuple-element.7.found, f32[512,128]{1,0:T(8,128)S(1)} %get-tuple-element.8.rows_in, f32[1,128]{1,0:T(1,128)S(1)} %get-tuple-element.9.total_in), custom_call_target="tpu_custom_call" | custom-call | tf_op jit(solution)/shard_map/adaptive_finish/pallas_call | solution.py:428
Async XLA Ops:
  0.6 0.7 %copy-start.2 = (s32[16]{0:T(128)S(1)}, s32[16]{0:T(128)}, u32[]{:S(2)}) copy-start(s32[16]{0:T(128)} %ids_hbm.1) | copy-start | bytes 196
  0.6 0.7 %copy-start.1 = (f32[8]{0:T(128)S(1)}, f32[8]{0:T(128)}, u32[]{:S(2)}) copy-start(f32[8]{0:T(128)} %table_hbm.1) | copy-start | bytes 100
  1.3 0.8 %copy-start = (s32[2,4096]{1,0:T(2,128)S(1)}, s32[2,4096]{1,0:T(2,128)}, u32[]{:S(2)}) copy-start(s32[2,4096]{1,0:T(2,128)} %mat_hbm.1) | copy-start | bytes 98308

commit v4 on v3

--- a/solution.py
+++ b/solution.py
@@ -35,6 +35,7 @@
     found = [()]
     for axis in step:
         found = [f + ((axis, d),) for f in found for d in range(axis[1])]
+    found.sort(key=lambda f: -sum(min(d, size - d) for (_, size), d in f))
     return [tuple(move for move in f if move[1]) for f in found if any(d for _, d in f)]
 
 

time: 56.2 us -> 56.2 us (level)
  no operation moved by 1% of the time
where the time goes in v4:
time: 56.2 us; the launch traced here: 56 us
  Pallas kernels  53.9 us (96%)
  local copies, waits for them, and re-layouts  1.41 us (3%)
  between operations  0.66 us (1%)
    pallas_call x1, Pallas kernels, local(): pl.pallas_call(functools.partial(kernel, n), out_shape=(jax.ShapeDtypeStr...  52.8 us
    unnamed x6, local copies, waits for them, and re-layouts  1.41 us

profile of v4, /device:TPU:32, one launch (start us, length us, event | category | flops | bytes accessed | tf_op | source)
XLA Modules:
  0.0 56.0 jit_solution(10107606356374516050)
XLA Ops:
  0.6 0.0 copy-start.2
  0.6 0.0 copy-start.1
  0.7 0.6 %copy-done.2 = s32[16]{0:T(128)S(1)} copy-done((s32[16]{0:T(128)S(1)}, s32[16]{0:T(128)}, u32[]{:S(2)}) %copy-start.2) | copy-done | bytes 88
  1.3 0.0 copy-done.1
  1.3 0.0 copy-start
  1.3 0.8 %copy-done = s32[2,4096]{1,0:T(2,128)S(1)} copy-done((s32[2,4096]{1,0:T(2,128)S(1)}, s32[2,4096]{1,0:T(2,128)}, u32[]{:S(2)}) %copy-start) | copy-done | bytes 32792
  2.1 52.8 %adaptive_setup.1 = (f32[2048,128]{1,0:T(8,128)S(1)}, f32[512,128]{1,0:T(8,128)S(1)}, f32[1,128]{1,0:T(1,128)S(1)}) custom-call(f32[2048,128]{1,0:T(8,128)} %bitcast.10, s32[2,4096]{1,0:T(2,128)S(1)} %copy-done, f32[8]{0:T(128)S(1)} %copy-done.1, s32[16]{0:T(128)S(1)} %copy-done.2), custom_call_target="tpu_custom_call" | custom-call | tf_op jit(solution)/shard_map/adaptive_setup/pallas_call | solution.py:386
  54.9 1.1 %adaptive_finish.1 = (f32[2048,128]{1,0:T(8,128)}, f32[16,32,32]{2,1,0:T(8,128)}) custom-call(f32[2048,128]{1,0:T(8,128)S(1)} %get-tuple-element.7.found, f32[512,128]{1,0:T(8,128)S(1)} %get-tuple-element.8.rows_in, f32[1,128]{1,0:T(1,128)S(1)} %get-tuple-element.9.total_in), custom_call_target="tpu_custom_call" | custom-call | tf_op jit(solution)/shard_map/adaptive_finish/pallas_call | solution.py:429
Async XLA Ops:
  0.6 0.7 %copy-start.2 = (s32[16]{0:T(128)S(1)}, s32[16]{0:T(128)}, u32[]{:S(2)}) copy-start(s32[16]{0:T(128)} %ids_hbm.1) | copy-start | bytes 196
  0.6 0.7 %copy-start.1 = (f32[8]{0:T(128)S(1)}, f32[8]{0:T(128)}, u32[]{:S(2)}) copy-start(f32[8]{0:T(128)} %table_hbm.1) | copy-start | bytes 100
  1.3 0.8 %copy-start = (s32[2,4096]{1,0:T(2,128)S(1)}, s32[2,4096]{1,0:T(2,128)}, u32[]{:S(2)}) copy-start(s32[2,4096]{1,0:T(2,128)} %mat_hbm.1) | copy-start | bytes 98308

commit v5 on v4

--- a/solution.py
+++ b/solution.py
@@ -341,8 +341,6 @@
         for t in range(BLKR // 128):
             out[pl.ds((c * (BLKR // 128) + t) * PLANES + z, K, stride=PLANE // 128 * PLANES), :] = p[:, t * 128 : (t + 1) * 128]
 
-    total[...] = reduce_recv(2)
-
     for i in range(3):
         for z in range(PLANES):
             sent(z, functools.partial(small_copy, z, i))
@@ -356,6 +354,8 @@
         return carry
 
     lax.fori_loop(0, SWEEPS * GROUPS, drain, 0)
+
+    total[...] = reduce_recv(2)
 
 
 def finish(found, rows_in, total_in, out, coarse, rows, total, scaled, sem):

time: 56.2 us -> 56 us (level)
  no operation moved by 1% of the time
where the time goes in v5:
time: 56 us; the launch traced here: 55.8 us
  Pallas kernels  53.7 us (96%)
  local copies, waits for them, and re-layouts  1.41 us (3%)
  between operations  0.66 us (1%)
    pallas_call x1, Pallas kernels, local(): pl.pallas_call(functools.partial(kernel, n), out_shape=(jax.ShapeDtypeStr...  52.6 us
    unnamed x6, local copies, waits for them, and re-layouts  1.41 us

profile of v5, /device:TPU:32, one launch (start us, length us, event | category | flops | bytes accessed | tf_op | source)
XLA Modules:
  0.0 55.8 jit_solution(17192793851836751647)
XLA Ops:
  0.6 0.0 copy-start.2
  0.6 0.0 copy-start.1
  0.7 0.6 %copy-done.2 = s32[16]{0:T(128)S(1)} copy-done((s32[16]{0:T(128)S(1)}, s32[16]{0:T(128)}, u32[]{:S(2)}) %copy-start.2) | copy-done | bytes 88
  1.3 0.0 copy-done.1
  1.3 0.0 copy-start
  1.3 0.8 %copy-done = s32[2,4096]{1,0:T(2,128)S(1)} copy-done((s32[2,4096]{1,0:T(2,128)S(1)}, s32[2,4096]{1,0:T(2,128)}, u32[]{:S(2)}) %copy-start) | copy-done | bytes 32792
  2.1 52.6 %adaptive_setup.1 = (f32[2048,128]{1,0:T(8,128)S(1)}, f32[512,128]{1,0:T(8,128)S(1)}, f32[1,128]{1,0:T(1,128)S(1)}) custom-call(f32[2048,128]{1,0:T(8,128)} %bitcast.10, s32[2,4096]{1,0:T(2,128)S(1)} %copy-done, f32[8]{0:T(128)S(1)} %copy-done.1, s32[16]{0:T(128)S(1)} %copy-done.2), custom_call_target="tpu_custom_call" | custom-call | tf_op jit(solution)/shard_map/adaptive_setup/pallas_call | solution.py:386
  54.7 1.1 %adaptive_finish.1 = (f32[2048,128]{1,0:T(8,128)}, f32[16,32,32]{2,1,0:T(8,128)}) custom-call(f32[2048,128]{1,0:T(8,128)S(1)} %get-tuple-element.7.found, f32[512,128]{1,0:T(8,128)S(1)} %get-tuple-element.8.rows_in, f32[1,128]{1,0:T(1,128)S(1)} %get-tuple-element.9.total_in), custom_call_target="tpu_custom_call" | custom-call | tf_op jit(solution)/shard_map/adaptive_finish/pallas_call | solution.py:429
Async XLA Ops:
  0.6 0.7 %copy-start.2 = (s32[16]{0:T(128)S(1)}, s32[16]{0:T(128)}, u32[]{:S(2)}) copy-start(s32[16]{0:T(128)} %ids_hbm.1) | copy-start | bytes 196
  0.6 0.7 %copy-start.1 = (f32[8]{0:T(128)S(1)}, f32[8]{0:T(128)}, u32[]{:S(2)}) copy-start(f32[8]{0:T(128)} %table_hbm.1) | copy-start | bytes 100
  1.3 0.8 %copy-start = (s32[2,4096]{1,0:T(2,128)S(1)}, s32[2,4096]{1,0:T(2,128)}, u32[]{:S(2)}) copy-start(s32[2,4096]{1,0:T(2,128)} %mat_hbm.1) | copy-start | bytes 98308
